TPU v7x, 32 devices: a whole 2x2x4 slice. The times are simulated.
32 devices in a mesh: groups: 2 (over y), frame: 4 (over z), head: 2 (over x), sub: 2 (over core).
Axes of the slice: x: 2, y: 2, z: 4, core: 2. Of those that a mesh axis runs over, the one named last changes fastest.
Arguments:
- queries: bfloat16 [3072, 2560], P(('groups', 'frame'), ('head', 'sub')), parts along dimension 0, may hold values from -6 to 6, as said below
- keyvals: bfloat16 [2, 3072, 2560], P(None, ('groups', 'frame'), ('head', 'sub')), parts along dimension 1, may hold values from -6 to 6, as said below
- residual_in: float32 [3072, 5120], P(('groups', 'frame'), ('head', 'sub')), parts along dimension 0, may hold values from -3 to 3
- gate: float32 [10240], P(('groups', 'head', 'sub')), parts along dimension 0, may hold values from -4 to 4
- out_weight: bfloat16 [2560, 5120], P(('head', 'sub'), 'frame'), may hold values from -0.125 to 0.125
- pattern: int32 [48, 8], P(('groups', 'frame')), parts along dimension 0, may hold values from 0 to 23, as said below
- live: int32 [48], P(('groups', 'frame')), parts along dimension 0, may hold values from 4 to 8
Outputs:
- updated: float32 [3072, 5120], P(('groups', 'frame'), ('head', 'sub')), parts along dimension 0
There are 2 independent parts, one for each index of `groups`. A program takes and returns all parts, laid end to end along the dimension named above; an argument that names none is the same for every part. Nothing has to cross between parts.
Inputs may be any that keep to these rules, and one draw needn't show every extreme that they name: `pattern`: entry 0 of each row is the query tile itself; entries below live of that row are distinct tiles lying in the query tile's frame or one frame before or after it; later entries repeat the query tile. `queries`: values of order one. `keyvals`: values of order one.
All inputs are finite; a program needn't handle non-finite values.
Results may differ from a plain program's by a relative error of at most 0.0065.
Values may be sent and summed in bfloat16 or wider, within the bound.
A program may use at most 128 MiB of HBM per device.

v0:
```python
import math

import jax
import jax.numpy as jnp
from jax import lax
from jax.sharding import PartitionSpec as P

HEAD_DIM = 128
TILES_F = 6
KSEL = 8


def padded_2(block, sides, width):
    for axis, dim in sides:
        count = lax.axis_size(axis)
        forward = [(i, i + 1) for i in range(count - 1)]
        backward = [(target, source) for source, target in forward]
        low = lax.ppermute(
            lax.slice_in_dim(block, block.shape[dim] - width, None, axis=dim), axis, forward
        )
        high = lax.ppermute(lax.slice_in_dim(block, 0, width, axis=dim), axis, backward)
        block = jnp.concatenate([low, block, high], axis=dim)
    return block


def per_device(queries, keyvals, residual_in, gate, out_weight, pattern, live):
    rows, width = queries.shape
    tile_count = pattern.shape[0]
    tile_rows = rows // tile_count
    head_count = width // HEAD_DIM
    padded = padded_2(keyvals, (("frame", 1),), TILES_F * tile_rows)
    first_tile = lax.axis_index("frame") * tile_count - TILES_F
    local_ids = pattern - first_tile
    key_tiles = padded.reshape(2, -1, tile_rows, width)
    picked = key_tiles[:, local_ids]
    picked = picked.reshape(2, tile_count, KSEL * tile_rows, head_count, HEAD_DIM)
    query_tiles = queries.reshape(tile_count, tile_rows, head_count, HEAD_DIM)
    scores = jnp.einsum(
        "tqhd,tkhd->thqk", query_tiles, picked[0], preferred_element_type=jnp.float32
    ) * (1.0 / math.sqrt(HEAD_DIM))
    slot = jnp.arange(KSEL * tile_rows, dtype=jnp.int32) // tile_rows
    allowed = slot[None, :] < live[:, None]
    scores = jnp.where(allowed[:, None, None, :], scores, -1e30)
    row_max = jnp.max(scores, axis=-1, keepdims=True)
    expo = jnp.exp(scores - row_max)
    probs = (expo / jnp.sum(expo, axis=-1, keepdims=True)).astype(jnp.bfloat16)
    attended = jnp.einsum(
        "thqk,tkhd->tqhd", probs, picked[1], preferred_element_type=jnp.float32
    ).astype(jnp.bfloat16)
    attended = attended.reshape(rows, width)
    partial_rows = jnp.dot(
        attended,
        lax.all_gather(out_weight, "frame", axis=1, tiled=True),
        preferred_element_type=jnp.float32,
    )
    summed = lax.psum_scatter(
        partial_rows.astype(jnp.bfloat16), ("head", "sub"), scatter_dimension=1, tiled=True
    ).astype(jnp.float32)
    return residual_in + gate[None, :] * summed


def solution(mesh):
    in_specs = (
        P(("groups", "frame"), ("head", "sub")),
        P(None, ("groups", "frame"), ("head", "sub")),
        P(("groups", "frame"), ("head", "sub")),
        P(("groups", "head", "sub")),
        P(("head", "sub"), "frame"),
        P(("groups", "frame"), None),
        P(("groups", "frame")),
    )
    out_specs = P(("groups", "frame"), ("head", "sub"))
    return jax.shard_map(
        per_device, mesh=mesh, in_specs=in_specs, out_specs=out_specs, check_vma=False
    )
```

profile of v0, /device:TPU:3, one launch (start us, length us, event | category | flops | bytes accessed | tf_op | source)
XLA Modules:
  0.0 201.7 jit_solution(16965201183154617614)
XLA Ops:
  6.5 0.7 all-gather.2.cloned.1.call-update
  7.3 3.3 %collective-permute-start = (bf16[2,384,640]{2,1,0:T(8,128)(2,1)}, bf16[2,384,640]{2,1,0:T(8,128)(2,1)S(1)}, u32[]{:S(2)}, u32[]{:S(2)}) collective-permute-start(bf16[2,384,640]{2,1,0:T(8,128)(2,1)} %param.8), channel_id=1, source_target_pairs={{0,4},{4,8},{8,12},{1,5},{5,9},{9,13},{2,6},{6,10},{10,14},{3,7},{... | collective-permute-start | bytes 2949128 | tf_op jit(solution)/shard_map/ppermute | solution.py:18
  10.6 1.3 collective-permute-start.1
  11.9 0.7 compare_select_fusion
  12.7 2.4 %reshape.54 = bf16[6,64,5,128]{3,2,1,0:T(8,128)(2,1)} reshape(bf16[384,640]{1,0:T(8,128)(2,1)} %param.7) | data formatting | bytes 983040 | tf_op jit(solution)/shard_map/reshape | solution.py:37
  15.0 0.7 broadcast_compare_fusion
  15.8 26.3 %collective-permute-done = bf16[2,384,640]{2,1,0:T(8,128)(2,1)S(1)} collective-permute-done((bf16[2,384,640]{2,1,0:T(8,128)(2,1)}, bf16[2,384,640]{2,1,0:T(8,128)(2,1)S(1)}, u32[]{:S(2)}, u32[]{:S(2)}) %collective-permute-start) | collective-permute-done | bytes 983072 | tf_op jit(solution)/shard_map/ppermute | solution.py:18
  42.1 0.9 copy-done.2
  43.0 16.4 %collective-permute-done.1 = bf16[2,384,640]{2,1,0:T(8,128)(2,1)} collective-permute-done((bf16[2,384,640]{2,1,0:T(8,128)(2,1)}, bf16[2,384,640]{2,1,0:T(8,128)(2,1)}, u32[]{:S(2)}, u32[]{:S(2)}) %collective-permute-start.1) | collective-permute-done | bytes 983072 | tf_op jit(solution)/shard_map/ppermute | solution.py:21
  59.4 2.0 %pad_maximum_fusion = bf16[2,1152,640]{2,1,0:T(8,128)(2,1)S(1)} fusion(bf16[2,384,640]{2,1,0:T(8,128)(2,1)} %collective-permute-done.1, bf16[2,384,640]{2,1,0:T(8,128)(2,1)} %param.8, bf16[2,384,640]{2,1,0:T(8,128)(2,1)} %copy-done.2), kind=kLoop, calls=%fused_computation.13 | loop fusion | flops 8847360 | bytes 5898240 | tf_op jit(solution)/shard_map/concatenate | solution.py:22
  61.5 6.0 %gather_fusion = bf16[48,2,64,640]{3,2,1,0:T(8,128)(2,1)} fusion(bf16[2,18,64,640]{3,2,1,0:T(8,128)(2,1)S(1)} %bitcast.27, s32[1024]{0:T(1024)S(1)} %pad_clamp_fusion), kind=kCustom, calls=%fused_computation | custom fusion | bytes 15728832 | tf_op jit(solution)/shard_map/gather | solution.py:35
  67.4 4.0 %copy.9 = bf16[48,2,64,640]{3,2,0,1:T(8,128)(2,1)S(1)} copy(bf16[48,2,64,640]{3,2,1,0:T(8,128)(2,1)} %gather_fusion) | data formatting | bytes 15728640 | tf_op jit(solution)/shard_map/gather | solution.py:35
  71.5 3.5 %fusion.27 = (bf16[1,6,8,64,640]{4,3,2,1,0:T(8,128)(2,1)}, bf16[1,6,8,64,640]{4,3,2,1,0:T(8,128)(2,1)}) fusion(bf16[2,6,8,64,640]{4,3,2,1,0:T(8,128)(2,1)S(1)} %bitcast.28), kind=kLoop, calls=%fused_computation.36 | loop fusion | bytes 15728640 | tf_op jit(solution)/shard_map/slice | solution.py:39
  75.0 9.6 %squeeze.7 = bf16[6,512,5,128]{3,2,1,0:T(8,128)(2,1)} reshape(bf16[1,6,8,64,640]{4,3,2,1,0:T(8,128)(2,1)} %get-tuple-element.5) | data formatting | bytes 7864320 | tf_op jit(solution)/shard_map/squeeze | solution.py:39
  84.6 9.7 %squeeze.6 = bf16[6,512,5,128]{3,2,1,0:T(8,128)(2,1)} reshape(bf16[1,6,8,64,640]{4,3,2,1,0:T(8,128)(2,1)} %get-tuple-element.6) | data formatting | bytes 7864320 | tf_op jit(solution)/shard_map/squeeze | solution.py:48
  94.3 4.5 %fusion.5 = f32[6,5,512,64]{2,3,1,0:T(8,128)S(1)} fusion(bf16[6,512,5,128]{3,2,1,0:T(8,128)(2,1)} %squeeze.7, bf16[6,64,5,128]{3,2,1,0:T(8,128)(2,1)S(1)} %copy-done), kind=kOutput, calls=%fused_computation.9 | convolution fusion | flops 251658240 | bytes 8355840 | tf_op jit(solution)/shard_map/tqhd,tkhd->thqk/dot_general | solution.py:38
  98.8 1.8 fusion.28
  100.6 0.4 slice-done.1
  101.0 1.3 fusion.16
  102.3 0.4 copy.13
  102.7 40.7 %all-gather.2.cloned.1.call-done = bf16[640,5120]{1,0:T(8,128)(2,1)} async-done(((bf16[640,1280]{1,0:T(8,128)(2,1)}), bf16[640,5120]{1,0:T(8,128)(2,1)}) %all-gather.2.cloned.1.call-update) | async-done | bytes 6553616 | tf_op jit(solution)/shard_map/all_gather | solution.py:53
  143.3 7.6 %convolution_convert_fusion = bf16[384,5120]{1,0:T(8,128)(2,1)} fusion(bf16[640,5120]{1,0:T(8,128)(2,1)} %all-gather.2.cloned.1.call-done, bf16[48,8,5,128]{3,2,1,0:T(8,128)(2,1)S(1)} %bitcast.31), kind=kOutput, calls=%fused_computation.2 | convolution fusion | flops 2518548480 | bytes 10977280 | tf_op jit(solution)/shard_map/dot_general | solution.py:51
  151.0 41.2 %reduce-scatter.2.cloned.1.call-done = bf16[384,1280]{1,0:T(8,128)(2,1)} async-done(((bf16[384,5120]{1,0:T(8,128)(2,1)}), bf16[384,1280]{1,0:T(8,128)(2,1)}) %reduce-scatter.2.cloned.1.call-update) | async-done | bytes 983056 | tf_op jit(solution)/shard_map/reduce_scatter | solution.py:56
  192.1 2.7 %multiply_add_fusion = f32[384,1280]{1,0:T(8,128)} fusion(f32[384,1280]{1,0:T(8,128)S(1)} %copy-done.1, bf16[384,1280]{1,0:T(8,128)(2,1)} %reduce-scatter.2.cloned.1.call-done, f32[1280]{0:T(1024)S(1)} %copy-done.3), kind=kLoop, calls=%fused_computation.14 | loop fusion | flops 1474560 | bytes 4920320 | tf_op jit(solution)/shard_map/add | solution.py:59
  (17 shorter events, 0.2 us)
Async XLA Ops:
  6.5 136.8 %all-gather.2.cloned.1.call-start = ((), (), s32[]{:S(2)}) async-start(), calls=%async_computation.1 | async-start | bytes 8192000 | tf_op jit(solution)/shard_map/all_gather | solution.py:53
  7.3 184.9 %reduce-scatter.2.cloned.1.call-start = ((), (), s32[]{:S(2)}) async-start(), calls=%async_computation.2 | async-start | bytes 4915200 | tf_op jit(solution)/shard_map/reduce_scatter | solution.py:56
  7.3 34.8 %collective-permute-start = (bf16[2,384,640]{2,1,0:T(8,128)(2,1)}, bf16[2,384,640]{2,1,0:T(8,128)(2,1)S(1)}, u32[]{:S(2)}, u32[]{:S(2)}) collective-permute-start(bf16[2,384,640]{2,1,0:T(8,128)(2,1)} %param.8), channel_id=1, source_target_pairs={{0,4},{4,8},{8,12},{1,5},{5,9},{9,13},{2,6},{6,10},{10,14},{3,7},{... | collective-permute-start | bytes 2949128 | tf_op jit(solution)/shard_map/ppermute | solution.py:18
  10.6 48.9 %collective-permute-start.1 = (bf16[2,384,640]{2,1,0:T(8,128)(2,1)}, bf16[2,384,640]{2,1,0:T(8,128)(2,1)}, u32[]{:S(2)}, u32[]{:S(2)}) collective-permute-start(bf16[2,384,640]{2,1,0:T(8,128)(2,1)} %param.8), channel_id=1, source_target_pairs={{4,0},{8,4},{12,8},{5,1},{9,5},{13,9},{6,2},{10,6},{14,10},{7,3},{... | collective-permute-start | bytes 2949128 | tf_op jit(solution)/shard_map/ppermute | solution.py:21
  42.1 0.9 copy-start.2
  84.6 9.7 %copy-start = (bf16[6,64,5,128]{3,2,1,0:T(8,128)(2,1)S(1)}, bf16[6,64,5,128]{3,2,1,0:T(8,128)(2,1)}, u32[]{:S(2)}) copy-start(bf16[6,64,5,128]{3,2,1,0:T(8,128)(2,1)} %reshape.54) | copy-start | bytes 1474564
  94.3 6.2 %slice-start = ((s8[6291456]{0:T(1024)(128)(4,1)}), s8[2097152]{0:T(1024)(128)(4,1)S(1)}, s32[]{:S(2)}) async-start(s8[6291456]{0:T(1024)(128)(4,1)} %bitcast.29), calls=%async_computation.3 | async-start | bytes 4194304
  98.8 2.2 %slice-start.1 = ((s8[6291456]{0:T(1024)(128)(4,1)}), s8[4194304]{0:T(1024)(128)(4,1)S(1)}, s32[]{:S(2)}) async-start(s8[6291456]{0:T(1024)(128)(4,1)} %bitcast.29), calls=%async_computation.4 | async-start | bytes 8388608
  150.9 41.2 %copy-start.1 = (f32[384,1280]{1,0:T(8,128)S(1)}, f32[384,1280]{1,0:T(8,128)}, u32[]{:S(2)}) copy-start(f32[384,1280]{1,0:T(8,128)} %param.9) | copy-start | bytes 5898244
  150.9 41.2 %copy-start.3 = (f32[1280]{0:T(1024)S(1)}, f32[1280]{0:T(1024)}, u32[]{:S(2)}) copy-start(f32[1280]{0:T(1024)} %param.10) | copy-start | bytes 15364
Sparse Core Ops, SparseCore 0:
  8.9 134.3 all-gather.1
  151.1 41.0 reduce-scatter.1
where the time goes:
time: 205 us; the launch traced here: 202 us
  waiting for transfers between devices  125 us (61%)
  local copies, waits for them, and re-layouts  37 us (18%)
  between operations  13.5 us (7%)
  matrix products  13.4 us (7%)
  other arithmetic  7.9 us (4%)
  starting transfers between devices  4.6 us (2%)
    reduce_scatter x1, waiting for transfers between devices, per_device(): lax.psum_scatter(partial_rows.astype(jnp.bfloat16), ('head', 'sub'), scat...  41.2 us
    all_gather x1, waiting for transfers between devices, per_device(): lax.all_gather(out_weight, 'frame', axis=1, tiled=True)  40.7 us
    ppermute x1, waiting for transfers between devices, padded_2(): lax.ppermute(lax.slice_in_dim(block, block.shape[dim] - width, None, axis...  26.3 us
    ppermute x1, waiting for transfers between devices, padded_2(): lax.ppermute(lax.slice_in_dim(block, 0, width, axis=dim), axis, backward)  16.4 us
    gather x2, local copies, waits for them, and re-layouts, per_device(): picked = key_tiles[:, local_ids]  9.99 us
    squeeze x1, local copies, waits for them, and re-layouts, per_device(): picked[1]  9.66 us
    squeeze x1, local copies, waits for them, and re-layouts, per_device(): picked[0]  9.62 us
    dot_general x1, matrix products, per_device(): jnp.dot(attended, lax.all_gather(out_weight, 'frame', axis=1, tiled=True)...  7.61 us
  transfers between devices with their start and end apart: 4, of which 4 were waited for; matrix products, arithmetic and copies ran while one was open for 23% of the time, Pallas kernels for 0%

commit v1 on v0

v1 whole, which is shorter than its diff:
```python
import functools
import math

import jax
import jax.numpy as jnp
from jax import lax
from jax.experimental import pallas as pl
from jax.experimental.pallas import tpu as pltpu
from jax.sharding import PartitionSpec as P

HEAD_DIM = 128
TILES_F = 6
KSEL = 8
COLS = 256
VMEM_LIMIT = 48 * 1024 * 1024
MESH = pl.DeviceIdType.MESH


def padded_2(block, axis, dim, width):
    count = lax.axis_size(axis)
    forward = [(i, i + 1) for i in range(count - 1)]
    backward = [(target, source) for source, target in forward]
    low = lax.ppermute(
        lax.slice_in_dim(block, block.shape[dim] - width, None, axis=dim), axis, forward
    )
    high = lax.ppermute(lax.slice_in_dim(block, 0, width, axis=dim), axis, backward)
    return jnp.concatenate([low, block, high], axis=dim)


def attend(first_tile, pattern_ref, live_ref, q_ref, kv_ref, att_ref):
    tile_count, tile_rows, width = q_ref.shape
    held = kv_ref.shape[1]
    scale = 1.0 / math.sqrt(HEAD_DIM)
    slot = lax.broadcasted_iota(jnp.int32, (tile_rows, KSEL * tile_rows), 1) // tile_rows

    def one_tile(t, carry):
        ids = [jnp.clip(pattern_ref[t, s] - first_tile, 0, held - 1) for s in range(KSEL)]
        keys = jnp.concatenate([kv_ref[0, i] for i in ids], axis=0)
        values = jnp.concatenate([kv_ref[1, i] for i in ids], axis=0)
        tile_queries = q_ref[t]
        allowed = slot < live_ref[t]
        for h in range(width // HEAD_DIM):
            cols = slice(h * HEAD_DIM, (h + 1) * HEAD_DIM)
            scores = lax.dot_general(
                tile_queries[:, cols],
                keys[:, cols],
                (((1,), (1,)), ((), ())),
                preferred_element_type=jnp.float32,
            )
            scores = jnp.where(allowed, scores * scale, -1e30)
            expo = jnp.exp(scores - jnp.max(scores, axis=-1, keepdims=True))
            probs = expo * (1.0 / jnp.sum(expo, axis=-1, keepdims=True))
            out = jnp.dot(
                probs.astype(jnp.bfloat16), values[:, cols], preferred_element_type=jnp.float32
            )
            rows = pl.ds(pl.multiple_of(t * tile_rows, tile_rows), tile_rows)
            att_ref[rows, cols] = out.astype(jnp.bfloat16)
        return carry

    lax.fori_loop(0, tile_count, one_tile, 0)


def attend_kernel(first_ref, pattern_ref, live_ref, q_ref, kv_ref, att_ref):
    attend(first_ref[0], pattern_ref, live_ref, q_ref, kv_ref, att_ref)


def plain_sum(queries, keyvals, out_weight, pattern, live):
    rows, width = queries.shape
    tile_count = pattern.shape[0]
    tile_rows = rows // tile_count
    padded = padded_2(keyvals, "frame", 1, TILES_F * tile_rows)
    first_tile = lax.axis_index("frame") * tile_count - TILES_F
    smem = pl.BlockSpec(memory_space=pltpu.SMEM)
    vmem = pl.BlockSpec(memory_space=pltpu.VMEM)
    attended = pl.pallas_call(
        attend_kernel,
        out_shape=jax.ShapeDtypeStruct((rows, width), jnp.bfloat16),
        in_specs=[smem, smem, smem, vmem, vmem],
        out_specs=vmem,
        compiler_params=pltpu.CompilerParams(vmem_limit_bytes=VMEM_LIMIT),
    )(
        jnp.reshape(first_tile, (1,)).astype(jnp.int32),
        pattern,
        live,
        queries.reshape(tile_count, tile_rows, width),
        padded.reshape(2, -1, tile_rows, width),
    )
    partial_rows = jnp.dot(
        attended,
        lax.all_gather(out_weight, "frame", axis=1, tiled=True),
        preferred_element_type=jnp.float32,
    )
    return lax.psum_scatter(
        partial_rows.astype(jnp.bfloat16), ("head", "sub"), scatter_dimension=1, tiled=True
    ).astype(jnp.float32)


def fused_kernel(
    frames, pattern_ref, live_ref, q_ref, kv_ref, w_ref, out_ref,
    kvbuf, wbuf, att, tmp, coresend, corebuf, xsend, xbuf,
    own_sem, halo_send, halo_recv, right_send, left_send, w_recv, y_send, y_recv,
    core_send, core_recv, x_send, x_recv,
):
    g, f = lax.axis_index("groups"), lax.axis_index("frame")
    x, core = lax.axis_index("head"), lax.axis_index("sub")
    tiles = q_ref.shape[0]
    depth, span = w_ref.shape
    half = depth // 2
    last = frames - 1
    to_left, to_right = {"frame": f - 1}, {"frame": f + 1}
    to_y, to_core, to_x = {"groups": 1 - g}, {"sub": 1 - core}, {"head": 1 - x}
    mine = pl.ds(pl.multiple_of(g * half, half), half)
    other = pl.ds(pl.multiple_of((1 - g) * half, half), half)

    barrier = pltpu.get_barrier_semaphore()

    def greet(where):
        pl.semaphore_signal(barrier, inc=1, device_id=where, device_id_type=MESH)

    for where in (to_y, to_core, to_x):
        greet(where)
    pl.when(f > 0)(lambda: greet(to_left))
    pl.when(f < last)(lambda: greet(to_right))
    ends = jnp.where(f > 0, 1, 0) + jnp.where(f < last, 1, 0)
    pl.semaphore_wait(barrier, 3 + ends)

    def remote(src, dst, send, recv, where):
        return pltpu.make_async_remote_copy(
            src_ref=src, dst_ref=dst, send_sem=send, recv_sem=recv,
            device_id=where, device_id_type=MESH,
        )

    own = pltpu.make_async_copy(kv_ref, kvbuf.at[:, pl.ds(tiles, tiles)], own_sem)
    low, high = kvbuf.at[:, pl.ds(0, tiles)], kvbuf.at[:, pl.ds(2 * tiles, tiles)]
    halo_right = remote(kv_ref, low, halo_send.at[0], halo_recv.at[0], to_right)
    halo_left = remote(kv_ref, high, halo_send.at[1], halo_recv.at[1], to_left)

    def along(chunk, where, sems, first=False):
        piece = wbuf.at[chunk, mine]
        return remote(
            w_ref.at[mine] if first else piece, piece, sems.at[chunk], w_recv.at[chunk], where
        )

    def across(chunk):
        piece = wbuf.at[chunk, mine]
        return remote(piece, piece, y_send.at[chunk], y_recv.at[chunk], to_y)

    pl.when(f < last)(halo_right.start)
    pl.when(f > 0)(halo_left.start)
    pl.when(f < last)(along(f, to_right, right_send, True).start)
    pl.when(f > 0)(along(f, to_left, left_send, True).start)
    own.start()

    def arrive(distance):
        @pl.when(f >= distance)
        def _():
            chunk = f - distance
            along(chunk, to_right, right_send).wait_recv()
            pl.when(f < last)(along(chunk, to_right, right_send).start)
            across(chunk).start()

        @pl.when(f + distance <= last)
        def _():
            chunk = f + distance
            along(chunk, to_left, left_send).wait_recv()
            pl.when(f > 0)(along(chunk, to_left, left_send).start)
            across(chunk).start()

    own.wait()
    pl.when(f > 0)(halo_right.wait_recv)
    pl.when(f < last)(halo_left.wait_recv)
    arrive(1)
    attend(f * tiles - tiles, pattern_ref, live_ref, q_ref, kvbuf, att)

    def core_copy(slot):
        return remote(
            coresend.at[slot], corebuf.at[slot], core_send.at[slot], core_recv.at[slot], to_core
        )

    x_copy = remote(xsend, xbuf, x_send, x_recv, to_x)

    def each_tile(body):
        @pl.loop(0, span // COLS)
        def _(n):
            body(pl.ds(pl.multiple_of(n * COLS, COLS), COLS))

    def project(chunk, weights):
        slot, parity = chunk // 2, chunk % 2

        def term(cols):
            tmp[:, cols] = jnp.dot(
                att[...], weights[:, cols], preferred_element_type=jnp.float32
            )

        each_tile(term)

        @pl.when(parity != core)
        def _():
            def pack(cols):
                coresend[slot, :, cols] = tmp[:, cols].astype(jnp.bfloat16)

            each_tile(pack)
            core_copy(slot).start()

        @pl.when(parity == core)
        def _():
            core_copy(slot).wait_recv()

            @pl.when(slot == x)
            def _():
                def keep(cols):
                    out_ref[:, cols] = tmp[:, cols] + corebuf[slot, :, cols].astype(jnp.float32)

                each_tile(keep)

            @pl.when(slot != x)
            def _():
                def pack(cols):
                    both = tmp[:, cols] + corebuf[slot, :, cols].astype(jnp.float32)
                    xsend[:, cols] = both.astype(jnp.bfloat16)

                each_tile(pack)
                x_copy.start()

    def step(chunk):
        piece = wbuf.at[chunk, other]
        remote(piece, piece, y_send.at[chunk], y_recv.at[chunk], to_y).wait_recv()
        project(chunk, wbuf.at[chunk])

    project(f, w_ref)
    for distance in range(1, frames):
        if distance + 1 < frames:
            arrive(distance + 1)
        pl.when(f >= distance)(lambda: step(f - distance))
        pl.when(f + distance <= last)(lambda: step(f + distance))

    x_copy.wait_recv()

    def finish(cols):
        out_ref[:, cols] = out_ref[:, cols] + xbuf[:, cols].astype(jnp.float32)

    each_tile(finish)

    x_copy.wait_send()
    for slot in range(2):
        core_copy(slot).wait_send()
    pl.when(f < last)(halo_right.wait_send)
    pl.when(f > 0)(halo_left.wait_send)
    pl.when(f < last)(along(f, to_right, right_send, True).wait_send)
    pl.when(f > 0)(along(f, to_left, left_send, True).wait_send)
    for distance in range(1, frames):

        @pl.when(f >= distance)
        def _():
            chunk = f - distance
            pl.when(f < last)(along(chunk, to_right, right_send).wait_send)
            across(chunk).wait_send()

        @pl.when(f + distance <= last)
        def _():
            chunk = f + distance
            pl.when(f > 0)(along(chunk, to_left, left_send).wait_send)
            across(chunk).wait_send()


def fused_sum(queries, keyvals, out_weight, pattern, live):
    rows, width = queries.shape
    frames = lax.axis_size("frame")
    tiles = pattern.shape[0]
    tile_rows = rows // tiles
    depth, span = out_weight.shape
    smem = pl.BlockSpec(memory_space=pltpu.SMEM)
    vmem = pl.BlockSpec(memory_space=pltpu.VMEM)
    dma = pltpu.SemaphoreType.DMA
    return pl.pallas_call(
        functools.partial(fused_kernel, frames),
        out_shape=jax.ShapeDtypeStruct((rows, span), jnp.float32),
        in_specs=[smem, smem, vmem, vmem, vmem],
        out_specs=vmem,
        scratch_shapes=[
            pltpu.VMEM((2, 3 * tiles, tile_rows, width), jnp.bfloat16),
            pltpu.VMEM((frames, depth, span), jnp.bfloat16),
            pltpu.VMEM((rows, width), jnp.bfloat16),
            pltpu.VMEM((rows, span), jnp.float32),
            pltpu.VMEM((2, rows, span), jnp.bfloat16),
            pltpu.VMEM((2, rows, span), jnp.bfloat16),
            pltpu.VMEM((rows, span), jnp.bfloat16),
            pltpu.VMEM((rows, span), jnp.bfloat16),
            dma(()), dma((2,)), dma((2,)), dma((frames,)), dma((frames,)), dma((frames,)),
            dma((frames,)), dma((frames,)), dma((2,)), dma((2,)), dma(()), dma(()),
        ],
        compiler_params=pltpu.CompilerParams(
            collective_id=0, has_side_effects=True, vmem_limit_bytes=VMEM_LIMIT
        ),
        cost_estimate=pl.CostEstimate(
            flops=2 * rows * depth * span * frames, bytes_accessed=8 << 20, transcendentals=1 << 20
        ),
    )(
        pattern,
        live,
        queries.reshape(tiles, tile_rows, width),
        keyvals.reshape(2, tiles, tile_rows, width),
        out_weight,
    )


def per_device(queries, keyvals, residual_in, gate, out_weight, pattern, live):
    size = lax.axis_size
    fits = (
        size("groups") == size("head") == size("sub") == 2
        and size("frame") == 4
        and pattern.shape[0] == TILES_F
        and out_weight.shape[0] % 32 == 0
        and out_weight.shape[1] % COLS == 0
    )
    total = fused_sum if fits else plain_sum
    return residual_in + gate[None, :] * total(queries, keyvals, out_weight, pattern, live)


def solution(mesh):
    in_specs = (
        P(("groups", "frame"), ("head", "sub")),
        P(None, ("groups", "frame"), ("head", "sub")),
        P(("groups", "frame"), ("head", "sub")),
        P(("groups", "head", "sub")),
        P(("head", "sub"), "frame"),
        P(("groups", "frame"), None),
        P(("groups", "frame")),
    )
    out_specs = P(("groups", "frame"), ("head", "sub"))
    return jax.shard_map(
        per_device, mesh=mesh, in_specs=in_specs, out_specs=out_specs, check_vma=False
    )
```

time: 205 us -> 121 us (0.59); the launches traced: 202 us -> 121 us
  waiting for transfers between devices: 125 us -> 0 us
  Pallas kernels: 0 us -> 114 us
  local copies, waits for them, and re-layouts: 37 us -> 5.01 us
  between operations: 13.5 us -> 0.03 us
  matrix products: 13.4 us -> 0 us
  other arithmetic: 7.9 us -> 1.5 us
  starting transfers between devices: 4.6 us -> 0 us
    pallas_call x0 -> x1, Pallas kernels: none -> 114 us  [fused_sum(): pl.pallas_call(functools.partial(fused_kernel, frames), out_shape=jax.Sha...]
    ppermute x2 -> x0, waiting for transfers between devices: 42.7 us -> none  [the longest x1 26.3 us: padded_2(): lax.ppermute(lax.slice_in_dim(block, block.shape[dim] - width, None, axis...]
    reduce_scatter x1 -> x0, waiting for transfers between devices: 41.2 us -> none  [per_device(): lax.psum_scatter(partial_rows.astype(jnp.bfloat16), ('head', 'sub'), scat...]
    all_gather x1 -> x0, waiting for transfers between devices: 40.7 us -> none  [per_device(): lax.all_gather(out_weight, 'frame', axis=1, tiled=True)]
    squeeze x2 -> x0, local copies, waits for them, and re-layouts: 19.3 us -> none  [the longest x1 9.66 us: per_device(): picked[1]]
    dot_general x3 -> x0, matrix products: 13.4 us -> none  [the longest x1 7.61 us: per_device(): jnp.dot(attended, lax.all_gather(out_weight, 'frame', axis=1, tiled=True)...]
    gather x2 -> x0, local copies, waits for them, and re-layouts: 9.99 us -> none  [per_device(): picked = key_tiles[:, local_ids]]
    ppermute x2 -> x0, starting transfers between devices: 4.56 us -> none  [the longest x1 3.26 us: padded_2(): lax.ppermute(lax.slice_in_dim(block, block.shape[dim] - width, None, axis...]
  transfers between devices with their start and end apart: 4 -> 0, of which waited for: 4 -> 0; matrix products, arithmetic and copies ran while one was open for 23% -> 0% of each run, Pallas kernels for 0% -> 0%
where the time goes in v1:
time: 121 us
  Pallas kernels  114 us (94%)
  local copies, waits for them, and re-layouts  5.01 us (4%)
  other arithmetic  1.5 us (1%)
    pallas_call x1, Pallas kernels, fused_sum(): pl.pallas_call(functools.partial(fused_kernel, frames), out_shape=jax.Sha...  114 us
    unnamed x14, local copies, waits for them, and re-layouts  5.01 us

profile of v1, /device:TPU:3, one launch (start us, length us, event | category | flops | bytes accessed | tf_op | source)
XLA Modules:
  0.0 121.0 jit_solution(12806756907585576568)
XLA Ops:
  0.0 0.0 copy-start
  0.0 1.4 %copy-done = bf16[640,1280]{1,0:T(8,128)(2,1)S(1)} copy-done((bf16[640,1280]{1,0:T(8,128)(2,1)S(1)}, bf16[640,1280]{1,0:T(8,128)(2,1)}, u32[]{:S(2)}) %copy-start) | copy-done | bytes 1638424
  1.4 0.0 copy-start.1
  1.4 1.2 copy-done.1
  2.6 0.0 copy-start.2
  2.6 1.0 copy-done.2
  3.7 0.0 copy-start.3
  3.7 0.7 copy-done.3
  4.4 0.0 copy-start.4
  4.4 0.7 copy-done.4
  5.0 0.0 copy-start.5
  5.0 0.0 copy-start.6
  5.0 114.5 %shard_map.73 = f32[384,1280]{1,0:T(8,128)S(1)} custom-call(s32[6,8]{1,0:T(8,128)S(1)} %copy-done.3, s32[6]{0:T(128)S(1)} %copy-done.4, bf16[6,64,640]{2,1,0:T(8,128)(2,1)S(1)} %bitcast.3, bf16[2,6,64,640]{3,2,1,0:T(8,128)(2,1)S(1)} %bitcast.2, bf16[640,1280]{1,0:T(8,128)(2,1)S(1)} %copy-done), custom_call_target="tpu_custom_call" | custom-call | flops 2516582400 | bytes 8388608 | tf_op jit(solution)/shard_map/pallas_call | solution.py:275
  119.5 0.0 copy-done.5
  119.5 0.0 copy-done.6
  119.5 1.5 %multiply_add_fusion = f32[384,1280]{1,0:T(8,128)} fusion(f32[384,1280]{1,0:T(8,128)S(1)} %copy-done.5, f32[384,1280]{1,0:T(8,128)S(1)} %shard_map.73, f32[1280]{0:T(1024)S(1)} %copy-done.6), kind=kLoop, calls=%fused_computation | loop fusion | flops 983040 | bytes 5903360 | tf_op jit(solution)/shard_map/add | solution.py:317
Async XLA Ops:
  0.0 1.4 %copy-start = (bf16[640,1280]{1,0:T(8,128)(2,1)S(1)}, bf16[640,1280]{1,0:T(8,128)(2,1)}, u32[]{:S(2)}) copy-start(bf16[640,1280]{1,0:T(8,128)(2,1)} %w_ref.1) | copy-start | bytes 4915204
  1.4 1.2 copy-start.1
  2.6 1.0 copy-start.2
  3.7 0.7 copy-start.3
  4.4 0.7 copy-start.4
  5.0 114.5 %copy-start.5 = (f32[384,1280]{1,0:T(8,128)S(1)}, f32[384,1280]{1,0:T(8,128)}, u32[]{:S(2)}) copy-start(f32[384,1280]{1,0:T(8,128)} %param.9) | copy-start | bytes 5898244
  5.0 114.5 %copy-start.6 = (f32[1280]{0:T(1024)S(1)}, f32[1280]{0:T(1024)}, u32[]{:S(2)}) copy-start(f32[1280]{0:T(1024)} %param.10) | copy-start | bytes 15364

commit v2 on v1

v2 whole, which is shorter than its diff:
```python
import functools
import math

import jax
import jax.numpy as jnp
from jax import lax
from jax.experimental import pallas as pl
from jax.experimental.pallas import tpu as pltpu
from jax.sharding import PartitionSpec as P

HEAD_DIM = 128
TILES_F = 6
KSEL = 8
COLS = 256
VMEM_LIMIT = 48 * 1024 * 1024
FUSED_LIMIT = 60 * 1024 * 1024
MESH = pl.DeviceIdType.MESH


def padded_2(block, axis, dim, width):
    count = lax.axis_size(axis)
    forward = [(i, i + 1) for i in range(count - 1)]
    backward = [(target, source) for source, target in forward]
    low = lax.ppermute(
        lax.slice_in_dim(block, block.shape[dim] - width, None, axis=dim), axis, forward
    )
    high = lax.ppermute(lax.slice_in_dim(block, 0, width, axis=dim), axis, backward)
    return jnp.concatenate([low, block, high], axis=dim)


def attend(first_tile, pattern_ref, live_ref, q_ref, kv_ref, att_ref, between=None):
    tile_count, tile_rows, width = q_ref.shape
    held = kv_ref.shape[1]
    scale = 1.0 / math.sqrt(HEAD_DIM)
    slot = lax.broadcasted_iota(jnp.int32, (tile_rows, KSEL * tile_rows), 1) // tile_rows

    def one_tile(t, carry):
        ids = [jnp.clip(pattern_ref[t, s] - first_tile, 0, held - 1) for s in range(KSEL)]
        keys = jnp.concatenate([kv_ref[0, i] for i in ids], axis=0)
        values = jnp.concatenate([kv_ref[1, i] for i in ids], axis=0)
        tile_queries = q_ref[t]
        allowed = slot < live_ref[t]
        for h in range(width // HEAD_DIM):
            cols = slice(h * HEAD_DIM, (h + 1) * HEAD_DIM)
            scores = lax.dot_general(
                tile_queries[:, cols],
                keys[:, cols],
                (((1,), (1,)), ((), ())),
                preferred_element_type=jnp.float32,
            )
            scores = jnp.where(allowed, scores * scale, -1e30)
            expo = jnp.exp(scores - jnp.max(scores, axis=-1, keepdims=True))
            probs = expo * (1.0 / jnp.sum(expo, axis=-1, keepdims=True))
            out = jnp.dot(
                probs.astype(jnp.bfloat16), values[:, cols], preferred_element_type=jnp.float32
            )
            rows = pl.ds(pl.multiple_of(t * tile_rows, tile_rows), tile_rows)
            att_ref[rows, cols] = out.astype(jnp.bfloat16)
        if between is not None:
            between(t)
        return carry

    lax.fori_loop(0, tile_count, one_tile, 0)


def attend_kernel(first_ref, pattern_ref, live_ref, q_ref, kv_ref, att_ref):
    attend(first_ref[0], pattern_ref, live_ref, q_ref, kv_ref, att_ref)


def plain_sum(queries, keyvals, out_weight, pattern, live):
    rows, width = queries.shape
    tile_count = pattern.shape[0]
    tile_rows = rows // tile_count
    padded = padded_2(keyvals, "frame", 1, TILES_F * tile_rows)
    first_tile = lax.axis_index("frame") * tile_count - TILES_F
    smem = pl.BlockSpec(memory_space=pltpu.SMEM)
    vmem = pl.BlockSpec(memory_space=pltpu.VMEM)
    attended = pl.pallas_call(
        attend_kernel,
        out_shape=jax.ShapeDtypeStruct((rows, width), jnp.bfloat16),
        in_specs=[smem, smem, smem, vmem, vmem],
        out_specs=vmem,
        compiler_params=pltpu.CompilerParams(vmem_limit_bytes=VMEM_LIMIT),
    )(
        jnp.reshape(first_tile, (1,)).astype(jnp.int32),
        pattern,
        live,
        queries.reshape(tile_count, tile_rows, width),
        padded.reshape(2, -1, tile_rows, width),
    )
    partial_rows = jnp.dot(
        attended,
        lax.all_gather(out_weight, "frame", axis=1, tiled=True),
        preferred_element_type=jnp.float32,
    )
    return lax.psum_scatter(
        partial_rows.astype(jnp.bfloat16), ("head", "sub"), scatter_dimension=1, tiled=True
    ).astype(jnp.float32)


def fused_kernel(
    frames, pattern_ref, live_ref, q_hbm, kv_hbm, w_hbm, out_ref,
    q_ref, kvbuf, w_ref, wbuf, att, coresend, corebuf, xsend, xbuf,
    own_sem, halo_send, halo_recv, right_send, left_send, w_recv, y_send, y_recv,
    core_send, core_recv, x_send, x_recv,
):
    g, f = lax.axis_index("groups"), lax.axis_index("frame")
    x, core = lax.axis_index("head"), lax.axis_index("sub")
    tiles = q_ref.shape[0]
    depth, span = w_ref.shape
    pieces = span // COLS
    half = depth // 2
    last = frames - 1
    to_left, to_right = {"frame": f - 1}, {"frame": f + 1}
    to_y, to_core, to_x = {"groups": 1 - g}, {"sub": 1 - core}, {"head": 1 - x}
    mine = pl.ds(pl.multiple_of(g * half, half), half)
    other = pl.ds(pl.multiple_of((1 - g) * half, half), half)

    own = [
        pltpu.make_async_copy(kv_hbm, kvbuf.at[:, pl.ds(tiles, tiles)], own_sem.at[0]),
        pltpu.make_async_copy(q_hbm, q_ref, own_sem.at[1]),
        pltpu.make_async_copy(w_hbm, w_ref, own_sem.at[2]),
    ]
    for copy in own:
        copy.start()

    barrier = pltpu.get_barrier_semaphore()

    def greet(where):
        pl.semaphore_signal(barrier, inc=1, device_id=where, device_id_type=MESH)

    for where in (to_y, to_core, to_x):
        greet(where)
    pl.when(f > 0)(lambda: greet(to_left))
    pl.when(f < last)(lambda: greet(to_right))
    ends = jnp.where(f > 0, 1, 0) + jnp.where(f < last, 1, 0)
    pl.semaphore_wait(barrier, 3 + ends)

    def remote(src, dst, send, recv, where):
        return pltpu.make_async_remote_copy(
            src_ref=src, dst_ref=dst, send_sem=send, recv_sem=recv,
            device_id=where, device_id_type=MESH,
        )

    def columns(j):
        return pl.ds(pl.multiple_of(j * COLS, COLS), COLS)

    low, high = kvbuf.at[:, pl.ds(0, tiles)], kvbuf.at[:, pl.ds(2 * tiles, tiles)]
    halo_right = remote(kv_hbm, low, halo_send.at[0], halo_recv.at[0], to_right)
    halo_left = remote(kv_hbm, high, halo_send.at[1], halo_recv.at[1], to_left)

    def along(chunk, j, where, sems, first=False):
        piece = wbuf.at[chunk, mine, columns(j)]
        src = w_hbm.at[mine, columns(j)] if first else piece
        return remote(src, piece, sems.at[chunk, j], w_recv.at[chunk, j], where)

    def across(chunk, j, rows):
        piece = wbuf.at[chunk, rows, columns(j)]
        return remote(piece, piece, y_send.at[chunk, j], y_recv.at[chunk, j], to_y)

    def each_piece(body, start=0):
        def run(j, carry):
            body(j)
            return carry

        lax.fori_loop(start, pieces, run, 0)

    def launch(j):
        pl.when(f < last)(along(f, j, to_right, right_send, True).start)
        pl.when(f > 0)(along(f, j, to_left, left_send, True).start)

    def arrive(distance, j):
        @pl.when(f >= distance)
        def _():
            chunk = f - distance
            along(chunk, j, to_right, right_send).wait_recv()
            pl.when(f < last)(along(chunk, j, to_right, right_send).start)
            across(chunk, j, mine).start()

        @pl.when(f + distance <= last)
        def _():
            chunk = f + distance
            along(chunk, j, to_left, left_send).wait_recv()
            pl.when(f > 0)(along(chunk, j, to_left, left_send).start)
            across(chunk, j, mine).start()

    pl.when(f < last)(halo_right.start)
    pl.when(f > 0)(halo_left.start)
    launch(0)
    for copy in own:
        copy.wait()
    pl.when(f > 0)(halo_right.wait_recv)
    pl.when(f < last)(halo_left.wait_recv)
    each_piece(launch, 1)

    def between(t):
        pl.when(t < pieces)(lambda: arrive(1, t))

    attend(f * tiles - tiles, pattern_ref, live_ref, q_ref, kvbuf, att, between)

    def core_copy(slot, j):
        return remote(
            coresend.at[slot, :, columns(j)], corebuf.at[slot, :, columns(j)],
            core_send.at[slot, j], core_recv.at[slot, j], to_core,
        )

    def x_copy(j):
        return remote(
            xsend.at[:, columns(j)], xbuf.at[:, columns(j)], x_send.at[j], x_recv.at[j], to_x
        )

    def project(chunk, j, weights):
        slot, parity = chunk // 2, chunk % 2
        cols = columns(j)
        term = jnp.dot(att[...], weights[:, cols], preferred_element_type=jnp.float32)

        @pl.when(parity != core)
        def _():
            coresend[slot, :, cols] = term.astype(jnp.bfloat16)
            core_copy(slot, j).start()

        @pl.when(parity == core)
        def _():
            out_or_send = slot == x
            core_copy(slot, j).wait_recv()
            both = term + corebuf[slot, :, cols].astype(jnp.float32)

            @pl.when(out_or_send)
            def _():
                out_ref[:, cols] = both

            @pl.when(jnp.logical_not(out_or_send))
            def _():
                xsend[:, cols] = both.astype(jnp.bfloat16)
                x_copy(j).start()

    def step(distance, j):
        def one(chunk):
            across(chunk, j, other).wait_recv()
            project(chunk, j, wbuf.at[chunk])

        pl.when(f >= distance)(lambda: one(f - distance))
        pl.when(f + distance <= last)(lambda: one(f + distance))

    each_piece(lambda j: project(f, j, w_ref))
    for distance in range(1, last):

        def events(j):
            arrive(distance + 1, j)
            step(distance, j)
            if distance + 1 == last:
                pl.when(j >= 2)(lambda: step(last, j - 2))

        each_piece(events)
    each_piece(lambda j: step(last, j), pieces - 2)

    def finish(j):
        x_copy(j).wait_recv()
        cols = columns(j)
        out_ref[:, cols] = out_ref[:, cols] + xbuf[:, cols].astype(jnp.float32)

    each_piece(finish)

    pl.when(f < last)(halo_right.wait_send)
    pl.when(f > 0)(halo_left.wait_send)

    def drain(j):
        x_copy(j).wait_send()
        for slot in range(2):
            core_copy(slot, j).wait_send()
        pl.when(f < last)(along(f, j, to_right, right_send, True).wait_send)
        pl.when(f > 0)(along(f, j, to_left, left_send, True).wait_send)
        for distance in range(1, frames):

            @pl.when(f >= distance)
            def _():
                chunk = f - distance
                pl.when(f < last)(along(chunk, j, to_right, right_send).wait_send)
                across(chunk, j, mine).wait_send()

            @pl.when(f + distance <= last)
            def _():
                chunk = f + distance
                pl.when(f > 0)(along(chunk, j, to_left, left_send).wait_send)
                across(chunk, j, mine).wait_send()

    each_piece(drain)


def fused_sum(queries, keyvals, out_weight, pattern, live):
    rows, width = queries.shape
    frames = lax.axis_size("frame")
    tiles = pattern.shape[0]
    tile_rows = rows // tiles
    depth, span = out_weight.shape
    pieces = span // COLS
    smem = pl.BlockSpec(memory_space=pltpu.SMEM)
    vmem = pl.BlockSpec(memory_space=pltpu.VMEM)
    anywhere = pl.BlockSpec(memory_space=pl.ANY)
    dma = pltpu.SemaphoreType.DMA
    bf16 = jnp.bfloat16
    return pl.pallas_call(
        functools.partial(fused_kernel, frames),
        out_shape=jax.ShapeDtypeStruct((rows, span), jnp.float32),
        in_specs=[smem, smem, anywhere, anywhere, anywhere],
        out_specs=vmem,
        scratch_shapes=[
            pltpu.VMEM((tiles, tile_rows, width), bf16),
            pltpu.VMEM((2, 3 * tiles, tile_rows, width), bf16),
            pltpu.VMEM((depth, span), bf16),
            pltpu.VMEM((frames, depth, span), bf16),
            pltpu.VMEM((rows, width), bf16),
            pltpu.VMEM((2, rows, span), bf16),
            pltpu.VMEM((2, rows, span), bf16),
            pltpu.VMEM((rows, span), bf16),
            pltpu.VMEM((rows, span), bf16),
            dma((3,)), dma((2,)), dma((2,)),
            dma((frames, pieces)), dma((frames, pieces)), dma((frames, pieces)),
            dma((frames, pieces)), dma((frames, pieces)),
            dma((2, pieces)), dma((2, pieces)), dma((pieces,)), dma((pieces,)),
        ],
        compiler_params=pltpu.CompilerParams(
            collective_id=0, has_side_effects=True, vmem_limit_bytes=FUSED_LIMIT
        ),
        cost_estimate=pl.CostEstimate(
            flops=2 * rows * depth * span * frames, bytes_accessed=8 << 20, transcendentals=1 << 20
        ),
    )(
        pattern,
        live,
        queries.reshape(tiles, tile_rows, width),
        keyvals.reshape(2, tiles, tile_rows, width),
        out_weight,
    )


def per_device(queries, keyvals, residual_in, gate, out_weight, pattern, live):
    size = lax.axis_size
    fits = (
        size("groups") == size("head") == size("sub") == 2
        and size("frame") == 4
        and pattern.shape[0] == TILES_F
        and out_weight.shape[1] <= TILES_F * COLS
        and out_weight.shape[0] % 32 == 0
        and out_weight.shape[1] % COLS == 0
    )
    total = fused_sum if fits else plain_sum
    return residual_in + gate[None, :] * total(queries, keyvals, out_weight, pattern, live)


def solution(mesh):
    in_specs = (
        P(("groups", "frame"), ("head", "sub")),
        P(None, ("groups", "frame"), ("head", "sub")),
        P(("groups", "frame"), ("head", "sub")),
        P(("groups", "head", "sub")),
        P(("head", "sub"), "frame"),
        P(("groups", "frame"), None),
        P(("groups", "frame")),
    )
    out_specs = P(("groups", "frame"), ("head", "sub"))
    return jax.shard_map(
        per_device, mesh=mesh, in_specs=in_specs, out_specs=out_specs, check_vma=False
    )
```

time: 121 us -> 98.4 us (0.81)
  Pallas kernels: 114 us -> 94.6 us
  local copies, waits for them, and re-layouts: 5.01 us -> 0.01 us
  other arithmetic: 1.5 us -> 3.04 us
    pallas_call x1, Pallas kernels: 114 us -> 94.6 us  [fused_sum(): pl.pallas_call(functools.partial(fused_kernel, frames), out_shape=jax.Sha...]
    unnamed x14 -> x4, local copies, waits for them, and re-layouts: 5.01 us -> 0.01 us
    add x1, other arithmetic: 1.5 us -> 3.04 us  [per_device(): residual_in + gate[None, :] * total(queries, keyvals, out_weight, pattern...]
where the time goes in v2:
time: 98.4 us; the launch traced here: 97.7 us
  Pallas kernels  94.6 us (96%)
  other arithmetic  3.04 us (3%)
    pallas_call x1, Pallas kernels, fused_sum(): pl.pallas_call(functools.partial(fused_kernel, frames), out_shape=jax.Sha...  94.6 us
    add x1, other arithmetic, per_device(): residual_in + gate[None, :] * total(queries, keyvals, out_weight, pattern...  3.04 us

profile of v2, /device:TPU:3, one launch (start us, length us, event | category | flops | bytes accessed | tf_op | source)
XLA Modules:
  0.0 97.7 jit_solution(9087935723255593727)
XLA Ops:
  0.0 0.0 copy-start
  0.0 0.0 copy-start.1
  0.0 94.6 %shard_map.73 = f32[384,1280]{1,0:T(8,128)} custom-call(s32[6,8]{1,0:T(8,128)} %pattern_ref.1, s32[6]{0:T(128)} %live_ref.1, bf16[6,64,640]{2,1,0:T(8,128)(2,1)} %bitcast.3, bf16[2,6,64,640]{3,2,1,0:T(8,128)(2,1)} %bitcast.2, bf16[640,1280]{1,0:T(8,128)(2,1)} %w_hbm.1), custom_call_target="tpu_custom_call" | custom-call | flops 2516582400 | bytes 8388608 | tf_op jit(solution)/shard_map/pallas_call | solution.py:302
  94.6 0.0 copy-done
  94.6 0.0 copy-done.1
  94.6 3.0 %multiply_add_fusion = f32[384,1280]{1,0:T(8,128)} fusion(f32[384,1280]{1,0:T(8,128)S(1)} %copy-done, f32[384,1280]{1,0:T(8,128)} %shard_map.73, f32[1280]{0:T(1024)S(1)} %copy-done.1), kind=kLoop, calls=%fused_computation | loop fusion | flops 983040 | bytes 5903360 | tf_op jit(solution)/shard_map/add | solution.py:348
Async XLA Ops:
  0.0 94.6 %copy-start = (f32[384,1280]{1,0:T(8,128)S(1)}, f32[384,1280]{1,0:T(8,128)}, u32[]{:S(2)}) copy-start(f32[384,1280]{1,0:T(8,128)} %param.9) | copy-start | bytes 5898244
  0.0 94.6 %copy-start.1 = (f32[1280]{0:T(1024)S(1)}, f32[1280]{0:T(1024)}, u32[]{:S(2)}) copy-start(f32[1280]{0:T(1024)} %param.10) | copy-start | bytes 15364

commit v3 on v2

--- a/solution.py
+++ b/solution.py
@@ -169,32 +169,39 @@
         pl.when(f < last)(along(f, j, to_right, right_send, True).start)
         pl.when(f > 0)(along(f, j, to_left, left_send, True).start)
 
-    def arrive(distance, j):
+    def take(distance, j):
         @pl.when(f >= distance)
         def _():
-            chunk = f - distance
-            along(chunk, j, to_right, right_send).wait_recv()
-            pl.when(f < last)(along(chunk, j, to_right, right_send).start)
-            across(chunk, j, mine).start()
+            along(f - distance, j, to_right, right_send).wait_recv()
+            across(f - distance, j, mine).start()
 
         @pl.when(f + distance <= last)
         def _():
-            chunk = f + distance
-            along(chunk, j, to_left, left_send).wait_recv()
-            pl.when(f > 0)(along(chunk, j, to_left, left_send).start)
-            across(chunk, j, mine).start()
-
+            along(f + distance, j, to_left, left_send).wait_recv()
+            across(f + distance, j, mine).start()
+
+    def pass_on(distance, j):
+        rightward = jnp.logical_and(f >= distance, f < last)
+        leftward = jnp.logical_and(f + distance <= last, f > 0)
+        pl.when(rightward)(along(f - distance, j, to_right, right_send).start)
+        pl.when(leftward)(along(f + distance, j, to_left, left_send).start)
+
+    def arrive(distance, j):
+        take(distance, j)
+        pass_on(distance, j)
+
+    each_piece(launch)
     pl.when(f < last)(halo_right.start)
     pl.when(f > 0)(halo_left.start)
-    launch(0)
+    each_piece(lambda j: take(1, j))
     for copy in own:
         copy.wait()
     pl.when(f > 0)(halo_right.wait_recv)
     pl.when(f < last)(halo_left.wait_recv)
-    each_piece(launch, 1)
+    each_piece(lambda j: pass_on(1, j))
 
     def between(t):
-        pl.when(t < pieces)(lambda: arrive(1, t))
+        pl.when(t < pieces)(lambda: arrive(2, t))
 
     attend(f * tiles - tiles, pattern_ref, live_ref, q_ref, kvbuf, att, between)
 
@@ -243,16 +250,15 @@
         pl.when(f + distance <= last)(lambda: one(f + distance))
 
     each_piece(lambda j: project(f, j, w_ref))
-    for distance in range(1, last):
-
-        def events(j):
-            arrive(distance + 1, j)
-            step(distance, j)
-            if distance + 1 == last:
-                pl.when(j >= 2)(lambda: step(last, j - 2))
-
-        each_piece(events)
-    each_piece(lambda j: step(last, j), pieces - 2)
+    each_piece(lambda j: step(1, j))
+
+    def events(j):
+        arrive(3, j)
+        step(2, j)
+        pl.when(j >= 2)(lambda: step(3, j - 2))
+
+    each_piece(events)
+    each_piece(lambda j: step(3, j), pieces - 2)
 
     def finish(j):
         x_copy(j).wait_recv()

time: 98.4 us -> 102 us (1.037)
  Pallas kernels: 94.6 us -> 98.7 us
    pallas_call x1, Pallas kernels: 94.6 us -> 98.7 us  [fused_sum(): pl.pallas_call(functools.partial(fused_kernel, frames), out_shape=jax.Sha...]
where the time goes in v3:
time: 102 us
  Pallas kernels  98.7 us (97%)
  other arithmetic  3.04 us (3%)
    pallas_call x1, Pallas kernels, fused_sum(): pl.pallas_call(functools.partial(fused_kernel, frames), out_shape=jax.Sha...  98.7 us
    add x1, other arithmetic, per_device(): residual_in + gate[None, :] * total(queries, keyvals, out_weight, pattern...  3.04 us

profile of v3, /device:TPU:3, one launch (start us, length us, event | category | flops | bytes accessed | tf_op | source)
XLA Modules:
  0.0 101.8 jit_solution(3298690933666301953)
XLA Ops:
  0.0 0.0 copy-start
  0.0 0.0 copy-start.1
  0.0 98.7 %shard_map.73 = f32[384,1280]{1,0:T(8,128)} custom-call(s32[6,8]{1,0:T(8,128)} %pattern_ref.1, s32[6]{0:T(128)} %live_ref.1, bf16[6,64,640]{2,1,0:T(8,128)(2,1)} %bitcast.3, bf16[2,6,64,640]{3,2,1,0:T(8,128)(2,1)} %bitcast.2, bf16[640,1280]{1,0:T(8,128)(2,1)} %w_hbm.1), custom_call_target="tpu_custom_call" | custom-call | flops 2516582400 | bytes 8388608 | tf_op jit(solution)/shard_map/pallas_call | solution.py:308
  98.7 0.0 copy-done
  98.7 0.0 copy-done.1
  98.7 3.0 %multiply_add_fusion = f32[384,1280]{1,0:T(8,128)} fusion(f32[384,1280]{1,0:T(8,128)S(1)} %copy-done, f32[384,1280]{1,0:T(8,128)} %shard_map.73, f32[1280]{0:T(1024)S(1)} %copy-done.1), kind=kLoop, calls=%fused_computation | loop fusion | flops 983040 | bytes 5903360 | tf_op jit(solution)/shard_map/add | solution.py:354
Async XLA Ops:
  0.0 98.7 %copy-start = (f32[384,1280]{1,0:T(8,128)S(1)}, f32[384,1280]{1,0:T(8,128)}, u32[]{:S(2)}) copy-start(f32[384,1280]{1,0:T(8,128)} %param.9) | copy-start | bytes 5898244
  0.0 98.7 %copy-start.1 = (f32[1280]{0:T(1024)S(1)}, f32[1280]{0:T(1024)}, u32[]{:S(2)}) copy-start(f32[1280]{0:T(1024)} %param.10) | copy-start | bytes 15364

commit v4 on v2

--- a/solution.py
+++ b/solution.py
@@ -99,10 +99,10 @@
 
 
 def fused_kernel(
-    frames, pattern_ref, live_ref, q_hbm, kv_hbm, w_hbm, out_ref,
-    q_ref, kvbuf, w_ref, wbuf, att, coresend, corebuf, xsend, xbuf,
+    frames, pattern_ref, live_ref, gate_ref, q_hbm, kv_hbm, w_hbm, res_hbm, out_hbm,
+    res_ref, acc_ref, q_ref, kvbuf, w_ref, wbuf, att, coresend, corebuf, xsend, xbuf,
     own_sem, halo_send, halo_recv, right_send, left_send, w_recv, y_send, y_recv,
-    core_send, core_recv, x_send, x_recv,
+    core_send, core_recv, x_send, x_recv, out_sem,
 ):
     g, f = lax.axis_index("groups"), lax.axis_index("frame")
     x, core = lax.axis_index("head"), lax.axis_index("sub")
@@ -120,6 +120,7 @@
         pltpu.make_async_copy(kv_hbm, kvbuf.at[:, pl.ds(tiles, tiles)], own_sem.at[0]),
         pltpu.make_async_copy(q_hbm, q_ref, own_sem.at[1]),
         pltpu.make_async_copy(w_hbm, w_ref, own_sem.at[2]),
+        pltpu.make_async_copy(res_hbm, res_ref, own_sem.at[3]),
     ]
     for copy in own:
         copy.start()
@@ -227,7 +228,7 @@
 
             @pl.when(out_or_send)
             def _():
-                out_ref[:, cols] = both
+                acc_ref[:, cols] = both
 
             @pl.when(jnp.logical_not(out_or_send))
             def _():
@@ -254,10 +255,16 @@
         each_piece(events)
     each_piece(lambda j: step(last, j), pieces - 2)
 
+    def out_copy(j):
+        cols = columns(j)
+        return pltpu.make_async_copy(acc_ref.at[:, cols], out_hbm.at[:, cols], out_sem.at[j])
+
     def finish(j):
         x_copy(j).wait_recv()
         cols = columns(j)
-        out_ref[:, cols] = out_ref[:, cols] + xbuf[:, cols].astype(jnp.float32)
+        summed = acc_ref[:, cols] + xbuf[:, cols].astype(jnp.float32)
+        acc_ref[:, cols] = res_ref[:, cols] + gate_ref[:, cols] * summed
+        out_copy(j).start()
 
     each_piece(finish)
 
@@ -265,6 +272,7 @@
     pl.when(f > 0)(halo_left.wait_send)
 
     def drain(j):
+        out_copy(j).wait()
         x_copy(j).wait_send()
         for slot in range(2):
             core_copy(slot, j).wait_send()
@@ -287,7 +295,7 @@
     each_piece(drain)
 
 
-def fused_sum(queries, keyvals, out_weight, pattern, live):
+def fused(queries, keyvals, residual_in, gate, out_weight, pattern, live):
     rows, width = queries.shape
     frames = lax.axis_size("frame")
     tiles = pattern.shape[0]
@@ -302,9 +310,11 @@
     return pl.pallas_call(
         functools.partial(fused_kernel, frames),
         out_shape=jax.ShapeDtypeStruct((rows, span), jnp.float32),
-        in_specs=[smem, smem, anywhere, anywhere, anywhere],
-        out_specs=vmem,
+        in_specs=[smem, smem, vmem, anywhere, anywhere, anywhere, anywhere],
+        out_specs=anywhere,
         scratch_shapes=[
+            pltpu.VMEM((rows, span), jnp.float32),
+            pltpu.VMEM((rows, span), jnp.float32),
             pltpu.VMEM((tiles, tile_rows, width), bf16),
             pltpu.VMEM((2, 3 * tiles, tile_rows, width), bf16),
             pltpu.VMEM((depth, span), bf16),
@@ -314,10 +324,11 @@
             pltpu.VMEM((2, rows, span), bf16),
             pltpu.VMEM((rows, span), bf16),
             pltpu.VMEM((rows, span), bf16),
-            dma((3,)), dma((2,)), dma((2,)),
+            dma((4,)), dma((2,)), dma((2,)),
             dma((frames, pieces)), dma((frames, pieces)), dma((frames, pieces)),
             dma((frames, pieces)), dma((frames, pieces)),
             dma((2, pieces)), dma((2, pieces)), dma((pieces,)), dma((pieces,)),
+            dma((pieces,)),
         ],
         compiler_params=pltpu.CompilerParams(
             collective_id=0, has_side_effects=True, vmem_limit_bytes=FUSED_LIMIT
@@ -328,9 +339,11 @@
     )(
         pattern,
         live,
+        gate.reshape(1, span),
         queries.reshape(tiles, tile_rows, width),
         keyvals.reshape(2, tiles, tile_rows, width),
         out_weight,
+        residual_in,
     )
 
 
@@ -344,8 +357,10 @@
         and out_weight.shape[0] % 32 == 0
         and out_weight.shape[1] % COLS == 0
     )
-    total = fused_sum if fits else plain_sum
-    return residual_in + gate[None, :] * total(queries, keyvals, out_weight, pattern, live)
+    if fits:
+        return fused(queries, keyvals, residual_in, gate, out_weight, pattern, live)
+    summed = plain_sum(queries, keyvals, out_weight, pattern, live)
+    return residual_in + gate[None, :] * summed
 
 
 def solution(mesh):

time: 98.4 us -> 99 us (level)
  local copies, waits for them, and re-layouts: 0.01 us -> 4.24 us
  other arithmetic: 3.04 us -> 0 us
    add x1 -> x0, other arithmetic: 3.04 us -> none  [per_device(): residual_in + gate[None, :] * total(queries, keyvals, out_weight, pattern...]
    unnamed x4 -> x1, local copies, waits for them, and re-layouts: 0.01 us -> 2.94 us
    reshape x0 -> x1, local copies, waits for them, and re-layouts: none -> 1.29 us  [fused(): gate.reshape(1, span)]
where the time goes in v4:
time: 99 us; the launch traced here: 98.1 us
  Pallas kernels  93.9 us (95%)
  local copies, waits for them, and re-layouts  4.24 us (4%)
    pallas_call x1, Pallas kernels, fused(): pl.pallas_call(functools.partial(fused_kernel, frames), out_shape=jax.Sha...  93.9 us
    unnamed x1, local copies, waits for them, and re-layouts  2.94 us

profile of v4, /device:TPU:3, one launch (start us, length us, event | category | flops | bytes accessed | tf_op | source)
XLA Modules:
  0.0 98.1 jit_solution(4360904599191642469)
XLA Ops:
  0.0 1.3 %reshape.9.gate_ref = f32[1,1280]{1,0:T(1,128)} reshape(f32[1280]{0:T(1024)} %param.10) | data formatting | bytes 10240 | tf_op jit(solution)/shard_map/reshape | solution.py:342
  1.3 93.9 %shard_map.73 = f32[384,1280]{1,0:T(8,128)} custom-call(s32[6,8]{1,0:T(8,128)} %pattern_ref.1, s32[6]{0:T(128)} %live_ref.1, f32[1,1280]{1,0:T(1,128)} %reshape.9.gate_ref, bf16[6,64,640]{2,1,0:T(8,128)(2,1)} %bitcast.3, bf16[2,6,64,640]{3,2,1,0:T(8,128)(2,1)} %bitcast.2, bf16[640,1280]{1,0:T(8,128)(2,1)} %w_hbm.1, f32[384,1280]{1,0:T(8,128)} %res_hbm.1), custom_call_target="tpu_custom_call" | custom-call | flops 2516582400 | bytes 8388608 | tf_op jit(solution)/shard_map/pallas_call | solution.py:310
  95.2 2.9 %copy.9 = f32[384,1280]{1,0:T(8,128)} copy(f32[384,1280]{1,0:T(8,128)} %shard_map.73) | data formatting | bytes 3932160

commit v5 on v2

--- a/solution.py
+++ b/solution.py
@@ -11,7 +11,8 @@
 HEAD_DIM = 128
 TILES_F = 6
 KSEL = 8
-COLS = 256
+COLS = 128
+LAG = 3
 VMEM_LIMIT = 48 * 1024 * 1024
 FUSED_LIMIT = 60 * 1024 * 1024
 MESH = pl.DeviceIdType.MESH
@@ -186,15 +187,17 @@
 
     pl.when(f < last)(halo_right.start)
     pl.when(f > 0)(halo_left.start)
-    launch(0)
+    for j in range(2):
+        launch(j)
     for copy in own:
         copy.wait()
     pl.when(f > 0)(halo_right.wait_recv)
     pl.when(f < last)(halo_left.wait_recv)
-    each_piece(launch, 1)
+    each_piece(launch, 2)
 
     def between(t):
-        pl.when(t < pieces)(lambda: arrive(1, t))
+        for j in (2 * t, 2 * t + 1):
+            pl.when(j < pieces)(functools.partial(arrive, 1, j))
 
     attend(f * tiles - tiles, pattern_ref, live_ref, q_ref, kvbuf, att, between)
 
@@ -249,10 +252,10 @@
             arrive(distance + 1, j)
             step(distance, j)
             if distance + 1 == last:
-                pl.when(j >= 2)(lambda: step(last, j - 2))
+                pl.when(j >= LAG)(lambda: step(last, j - LAG))
 
         each_piece(events)
-    each_piece(lambda j: step(last, j), pieces - 2)
+    each_piece(lambda j: step(last, j), pieces - LAG)
 
     def finish(j):
         x_copy(j).wait_recv()
@@ -340,7 +343,7 @@
         size("groups") == size("head") == size("sub") == 2
         and size("frame") == 4
         and pattern.shape[0] == TILES_F
-        and out_weight.shape[1] <= TILES_F * COLS
+        and out_weight.shape[1] <= 2 * TILES_F * COLS
         and out_weight.shape[0] % 32 == 0
         and out_weight.shape[1] % COLS == 0
     )

time: 98.4 us -> 104 us (1.057)
  Pallas kernels: 94.6 us -> 99.5 us
    pallas_call x1, Pallas kernels: 94.6 us -> 99.5 us  [fused_sum(): pl.pallas_call(functools.partial(fused_kernel, frames), out_shape=jax.Sha...]
where the time goes in v5:
time: 104 us; the launch traced here: 103 us
  Pallas kernels  99.5 us (96%)
  other arithmetic  3.04 us (3%)
    pallas_call x1, Pallas kernels, fused_sum(): pl.pallas_call(functools.partial(fused_kernel, frames), out_shape=jax.Sha...  99.5 us
    add x1, other arithmetic, per_device(): residual_in + gate[None, :] * total(queries, keyvals, out_weight, pattern...  3.04 us

profile of v5, /device:TPU:3, one launch (start us, length us, event | category | flops | bytes accessed | tf_op | source)
XLA Modules:
  0.0 102.5 jit_solution(2157555372629485797)
XLA Ops:
  0.0 0.0 copy-start
  0.0 0.0 copy-start.1
  0.0 99.5 %shard_map.73 = f32[384,1280]{1,0:T(8,128)} custom-call(s32[6,8]{1,0:T(8,128)} %pattern_ref.1, s32[6]{0:T(128)} %live_ref.1, bf16[6,64,640]{2,1,0:T(8,128)(2,1)} %bitcast.3, bf16[2,6,64,640]{3,2,1,0:T(8,128)(2,1)} %bitcast.2, bf16[640,1280]{1,0:T(8,128)(2,1)} %w_hbm.1), custom_call_target="tpu_custom_call" | custom-call | flops 2516582400 | bytes 8388608 | tf_op jit(solution)/shard_map/pallas_call | solution.py:305
  99.5 0.0 copy-done
  99.5 0.0 copy-done.1
  99.5 3.0 %multiply_add_fusion = f32[384,1280]{1,0:T(8,128)} fusion(f32[384,1280]{1,0:T(8,128)S(1)} %copy-done, f32[384,1280]{1,0:T(8,128)} %shard_map.73, f32[1280]{0:T(1024)S(1)} %copy-done.1), kind=kLoop, calls=%fused_computation | loop fusion | flops 983040 | bytes 5903360 | tf_op jit(solution)/shard_map/add | solution.py:351
Async XLA Ops:
  0.0 99.5 %copy-start = (f32[384,1280]{1,0:T(8,128)S(1)}, f32[384,1280]{1,0:T(8,128)}, u32[]{:S(2)}) copy-start(f32[384,1280]{1,0:T(8,128)} %param.9) | copy-start | bytes 5898244
  0.0 99.5 %copy-start.1 = (f32[1280]{0:T(1024)S(1)}, f32[1280]{0:T(1024)}, u32[]{:S(2)}) copy-start(f32[1280]{0:T(1024)} %param.10) | copy-start | bytes 15364

commit v6 on v2

--- a/solution.py
+++ b/solution.py
@@ -99,10 +99,10 @@
 
 
 def fused_kernel(
-    frames, pattern_ref, live_ref, q_hbm, kv_hbm, w_hbm, out_ref,
-    q_ref, kvbuf, w_ref, wbuf, att, coresend, corebuf, xsend, xbuf,
+    frames, pattern_ref, live_ref, q_hbm, kv_hbm, w_hbm, out_hbm,
+    acc_ref, q_ref, kvbuf, w_ref, wbuf, att, coresend, corebuf, xsend, xbuf,
     own_sem, halo_send, halo_recv, right_send, left_send, w_recv, y_send, y_recv,
-    core_send, core_recv, x_send, x_recv,
+    core_send, core_recv, x_send, x_recv, out_sem,
 ):
     g, f = lax.axis_index("groups"), lax.axis_index("frame")
     x, core = lax.axis_index("head"), lax.axis_index("sub")
@@ -121,7 +121,7 @@
         pltpu.make_async_copy(q_hbm, q_ref, own_sem.at[1]),
         pltpu.make_async_copy(w_hbm, w_ref, own_sem.at[2]),
     ]
-    for copy in own:
+    for copy in reversed(own):
         copy.start()
 
     barrier = pltpu.get_barrier_semaphore()
@@ -151,7 +151,7 @@
 
     def along(chunk, j, where, sems, first=False):
         piece = wbuf.at[chunk, mine, columns(j)]
-        src = w_hbm.at[mine, columns(j)] if first else piece
+        src = w_ref.at[mine, columns(j)] if first else piece
         return remote(src, piece, sems.at[chunk, j], w_recv.at[chunk, j], where)
 
     def across(chunk, j, rows):
@@ -186,8 +186,9 @@
 
     pl.when(f < last)(halo_right.start)
     pl.when(f > 0)(halo_left.start)
+    own[2].wait()
     launch(0)
-    for copy in own:
+    for copy in own[:2]:
         copy.wait()
     pl.when(f > 0)(halo_right.wait_recv)
     pl.when(f < last)(halo_left.wait_recv)
@@ -227,7 +228,7 @@
 
             @pl.when(out_or_send)
             def _():
-                out_ref[:, cols] = both
+                acc_ref[:, cols] = both
 
             @pl.when(jnp.logical_not(out_or_send))
             def _():
@@ -254,10 +255,15 @@
         each_piece(events)
     each_piece(lambda j: step(last, j), pieces - 2)
 
+    def out_copy(j):
+        cols = columns(j)
+        return pltpu.make_async_copy(acc_ref.at[:, cols], out_hbm.at[:, cols], out_sem.at[j])
+
     def finish(j):
         x_copy(j).wait_recv()
         cols = columns(j)
-        out_ref[:, cols] = out_ref[:, cols] + xbuf[:, cols].astype(jnp.float32)
+        acc_ref[:, cols] = acc_ref[:, cols] + xbuf[:, cols].astype(jnp.float32)
+        out_copy(j).start()
 
     each_piece(finish)
 
@@ -265,6 +271,7 @@
     pl.when(f > 0)(halo_left.wait_send)
 
     def drain(j):
+        out_copy(j).wait()
         x_copy(j).wait_send()
         for slot in range(2):
             core_copy(slot, j).wait_send()
@@ -295,7 +302,6 @@
     depth, span = out_weight.shape
     pieces = span // COLS
     smem = pl.BlockSpec(memory_space=pltpu.SMEM)
-    vmem = pl.BlockSpec(memory_space=pltpu.VMEM)
     anywhere = pl.BlockSpec(memory_space=pl.ANY)
     dma = pltpu.SemaphoreType.DMA
     bf16 = jnp.bfloat16
@@ -303,8 +309,9 @@
         functools.partial(fused_kernel, frames),
         out_shape=jax.ShapeDtypeStruct((rows, span), jnp.float32),
         in_specs=[smem, smem, anywhere, anywhere, anywhere],
-        out_specs=vmem,
+        out_specs=anywhere,
         scratch_shapes=[
+            pltpu.VMEM((rows, span), jnp.float32),
             pltpu.VMEM((tiles, tile_rows, width), bf16),
             pltpu.VMEM((2, 3 * tiles, tile_rows, width), bf16),
             pltpu.VMEM((depth, span), bf16),
@@ -318,6 +325,7 @@
             dma((frames, pieces)), dma((frames, pieces)), dma((frames, pieces)),
             dma((frames, pieces)), dma((frames, pieces)),
             dma((2, pieces)), dma((2, pieces)), dma((pieces,)), dma((pieces,)),
+            dma((pieces,)),
         ],
         compiler_params=pltpu.CompilerParams(
             collective_id=0, has_side_effects=True, vmem_limit_bytes=FUSED_LIMIT

time: 98.4 us -> 97.8 us (level)
  no operation moved by 1% of the time
where the time goes in v6:
time: 97.8 us; the launch traced here: 97.1 us
  Pallas kernels  94 us (96%)
  other arithmetic  3.04 us (3%)
    pallas_call x1, Pallas kernels, fused_sum(): pl.pallas_call(functools.partial(fused_kernel, frames), out_shape=jax.Sha...  94 us
    add x1, other arithmetic, per_device(): residual_in + gate[None, :] * total(queries, keyvals, out_weight, pattern...  3.04 us

profile of v6, /device:TPU:3, one launch (start us, length us, event | category | flops | bytes accessed | tf_op | source)
XLA Modules:
  0.0 97.1 jit_solution(13011131937924160373)
XLA Ops:
  0.0 0.0 copy-start
  0.0 0.0 copy-start.1
  0.0 94.0 %shard_map.73 = f32[384,1280]{1,0:T(8,128)} custom-call(s32[6,8]{1,0:T(8,128)} %pattern_ref.1, s32[6]{0:T(128)} %live_ref.1, bf16[6,64,640]{2,1,0:T(8,128)(2,1)} %bitcast.3, bf16[2,6,64,640]{3,2,1,0:T(8,128)(2,1)} %bitcast.2, bf16[640,1280]{1,0:T(8,128)(2,1)} %w_hbm.1), custom_call_target="tpu_custom_call" | custom-call | flops 2516582400 | bytes 8388608 | tf_op jit(solution)/shard_map/pallas_call | solution.py:308
  94.0 0.0 copy-done
  94.0 0.0 copy-done.1
  94.0 3.0 %multiply_add_fusion = f32[384,1280]{1,0:T(8,128)} fusion(f32[384,1280]{1,0:T(8,128)S(1)} %copy-done, f32[384,1280]{1,0:T(8,128)} %shard_map.73, f32[1280]{0:T(1024)S(1)} %copy-done.1), kind=kLoop, calls=%fused_computation | loop fusion | flops 983040 | bytes 5903360 | tf_op jit(solution)/shard_map/add | solution.py:356
Async XLA Ops:
  0.0 94.0 %copy-start = (f32[384,1280]{1,0:T(8,128)S(1)}, f32[384,1280]{1,0:T(8,128)}, u32[]{:S(2)}) copy-start(f32[384,1280]{1,0:T(8,128)} %param.9) | copy-start | bytes 5898244
  0.0 94.0 %copy-start.1 = (f32[1280]{0:T(1024)S(1)}, f32[1280]{0:T(1024)}, u32[]{:S(2)}) copy-start(f32[1280]{0:T(1024)} %param.10) | copy-start | bytes 15364

commit v7 on v6

--- a/solution.py
+++ b/solution.py
@@ -12,6 +12,7 @@
 TILES_F = 6
 KSEL = 8
 COLS = 256
+AHEAD = 3
 VMEM_LIMIT = 48 * 1024 * 1024
 FUSED_LIMIT = 60 * 1024 * 1024
 MESH = pl.DeviceIdType.MESH
@@ -187,12 +188,13 @@
     pl.when(f < last)(halo_right.start)
     pl.when(f > 0)(halo_left.start)
     own[2].wait()
-    launch(0)
+    for j in range(AHEAD):
+        launch(j)
     for copy in own[:2]:
         copy.wait()
     pl.when(f > 0)(halo_right.wait_recv)
     pl.when(f < last)(halo_left.wait_recv)
-    each_piece(launch, 1)
+    each_piece(launch, AHEAD)
 
     def between(t):
         pl.when(t < pieces)(lambda: arrive(1, t))
@@ -348,7 +350,7 @@
         size("groups") == size("head") == size("sub") == 2
         and size("frame") == 4
         and pattern.shape[0] == TILES_F
-        and out_weight.shape[1] <= TILES_F * COLS
+        and AHEAD * COLS <= out_weight.shape[1] <= TILES_F * COLS
         and out_weight.shape[0] % 32 == 0
         and out_weight.shape[1] % COLS == 0
     )

time: 97.8 us -> 97.8 us (level)
  no operation moved by 1% of the time
where the time goes in v7:
time: 97.8 us; the launch traced here: 97.1 us
  Pallas kernels  94 us (96%)
  other arithmetic  3.04 us (3%)
    pallas_call x1, Pallas kernels, fused_sum(): pl.pallas_call(functools.partial(fused_kernel, frames), out_shape=jax.Sha...  94 us
    add x1, other arithmetic, per_device(): residual_in + gate[None, :] * total(queries, keyvals, out_weight, pattern...  3.04 us

profile of v7, /device:TPU:3, one launch (start us, length us, event | category | flops | bytes accessed | tf_op | source)
XLA Modules:
  0.0 97.1 jit_solution(9419064531391578967)
XLA Ops:
  0.0 0.0 copy-start
  0.0 0.0 copy-start.1
  0.0 94.0 %shard_map.73 = f32[384,1280]{1,0:T(8,128)} custom-call(s32[6,8]{1,0:T(8,128)} %pattern_ref.1, s32[6]{0:T(128)} %live_ref.1, bf16[6,64,640]{2,1,0:T(8,128)(2,1)} %bitcast.3, bf16[2,6,64,640]{3,2,1,0:T(8,128)(2,1)} %bitcast.2, bf16[640,1280]{1,0:T(8,128)(2,1)} %w_hbm.1), custom_call_target="tpu_custom_call" | custom-call | flops 2516582400 | bytes 8388608 | tf_op jit(solution)/shard_map/pallas_call | solution.py:310
  94.0 0.0 copy-done
  94.0 0.0 copy-done.1
  94.0 3.0 %multiply_add_fusion = f32[384,1280]{1,0:T(8,128)} fusion(f32[384,1280]{1,0:T(8,128)S(1)} %copy-done, f32[384,1280]{1,0:T(8,128)} %shard_map.73, f32[1280]{0:T(1024)S(1)} %copy-done.1), kind=kLoop, calls=%fused_computation | loop fusion | flops 983040 | bytes 5903360 | tf_op jit(solution)/shard_map/add | solution.py:358
Async XLA Ops:
  0.0 94.0 %copy-start = (f32[384,1280]{1,0:T(8,128)S(1)}, f32[384,1280]{1,0:T(8,128)}, u32[]{:S(2)}) copy-start(f32[384,1280]{1,0:T(8,128)} %param.9) | copy-start | bytes 5898244
  0.0 94.0 %copy-start.1 = (f32[1280]{0:T(1024)S(1)}, f32[1280]{0:T(1024)}, u32[]{:S(2)}) copy-start(f32[1280]{0:T(1024)} %param.10) | copy-start | bytes 15364
